TPU v7x, 32 devices: a whole 2x2x4 slice. The times are simulated.
32 devices in a mesh: seq: 8 (over y, x, core), tp: 4 (over z).
Axes of the slice: x: 2, y: 2, z: 4, core: 2. Of those that a mesh axis runs over, the one named last changes fastest.
Arguments:
- hidden_in: bfloat16 [2048, 2048], P(('seq', 'tp')), may hold values from -6 to 6
- attention_gain: float32 [2048], replicated, may hold values from 0.1 to 1.9
- attention_trainer_copy: float32 [2048, 5120], P(('seq', 'tp')), may hold values from -0.125 to 0.125
- query_gain: float32 [128], replicated, may hold values from 0.1 to 1.9
- key_gain: float32 [128], replicated, may hold values from 0.1 to 1.9
- output_proj: bfloat16 [4096, 2048], P('tp'), may hold values from -0.09375 to 0.09375
- post_gain: float32 [2048], replicated, may hold values from 0.1 to 1.9
- router_weight: bfloat16 [2048, 16], replicated, may hold values from -0.125 to 0.125
- gate_up_master: float32 [16, 2048, 1536], P(None, ('seq', 'tp')), may hold values from -0.125 to 0.125
- down_weight: bfloat16 [16, 768, 2048], P('seq', 'tp'), may hold values from -0.21875 to 0.21875
- routes: int32 [2048, 8], P(('seq', 'tp')), may hold values from 0 to 15, all different within a row; in each aligned block of 64 rows (0 to 63, 64 to 127, ...) at most 64 rows name the same one
- lengths: int32 [8], P('seq'), may hold values from 1 to 256, 1024 in all
- page_table: int32 [8, 2], P('seq'), may hold values from 0 to 3, as said below
Outputs:
- hidden_leaving: bfloat16 [2048, 2048], P(('seq', 'tp'))
- cache_pages: bfloat16 [32, 2, 4, 128, 128], P('seq', None, 'tp')
Inputs may be any that keep to these rules, and one draw needn't show every extreme that they name: `routes`: each row names 8 different experts. In each aligned block of 64 rows (the rows of one device) no expert is named by more than 64 rows, a bound that some block reaches. `lengths`: some prompt has exactly 256 live positions. `page_table`: the 2 slots of one prompt are distinct.
All inputs are finite; a program needn't handle non-finite values. No bound on the sum of `lengths` on one device may be relied on, other than what follows from the above.
Results may differ from a plain program's by a relative error of at most 0.0085.
Values may be sent and summed in bfloat16 or wider, within the bound.
A program may use at most 128 MiB of HBM per device.

v0:
```python
import math

import jax
import jax.numpy as jnp
from jax import lax
from jax.sharding import PartitionSpec as P

QUERY_HEADS = 32
KEY_VALUE_HEADS = 4
HEAD_SIZE = 128
FF = 768
TOPK = 8
PAGE_POSITIONS = 128


EPS = 1e-06
THETA = 1000000.0


def rms_scale(values, gain):
    return values * lax.rsqrt(jnp.mean(values * values, axis=-1, keepdims=True) + EPS) * gain


def rotate(values, positions):
    half_dim = values.shape[-1] // 2
    frequency = THETA ** (-2.0 * jnp.arange(half_dim, dtype=jnp.float32) / values.shape[-1])
    angles = positions.astype(jnp.float32)[:, None] * frequency[None, :]
    cosine = jnp.cos(angles)[:, None, :]
    sine = jnp.sin(angles)[:, None, :]
    first_half = values[..., :half_dim]
    second_half = values[..., half_dim:]
    return jnp.concatenate(
        [first_half * cosine - second_half * sine, second_half * cosine + first_half * sine],
        axis=-1,
    )


def attend_prompt(query_rows, keys_rotated, values_in, prompt_length):
    column_span = query_rows.shape[0]
    scores = jnp.einsum(
        "qhgd,khd->hgqk", query_rows, keys_rotated, preferred_element_type=jnp.float32
    ) / math.sqrt(query_rows.shape[-1])
    places = jnp.arange(column_span)
    allowed = (places[None, :] <= places[:, None]) & (places[None, :] < prompt_length)
    weights = jnp.where(allowed, jnp.exp(scores), 0.0)
    probs = (weights / jnp.sum(weights, axis=-1, keepdims=True)).astype(jnp.bfloat16)
    context_rows = jnp.einsum(
        "hgqk,khd->qhgd", probs, values_in, preferred_element_type=jnp.float32
    )
    return context_rows.astype(jnp.bfloat16).reshape(column_span, -1)


def regroup(features, seq_count, tensor_parallel_count):
    leading = features.shape[:-1]
    blocks = features.reshape(leading + (seq_count, tensor_parallel_count, -1))
    return jnp.swapaxes(blocks, -3, -2).reshape(leading + (-1,))


def on_device(
    hidden_in,
    attention_gain,
    attention_trainer_copy,
    query_gain,
    key_gain,
    output_proj,
    post_gain,
    router_weight,
    gate_up_master,
    down_weight,
    routes,
    lengths,
    page_table,
):
    tensor_parallel_count = lax.axis_size("tp")
    seq_count = lax.axis_size("seq")
    tp_place = lax.axis_index("tp")
    quarter = hidden_in.shape[0]
    width = hidden_in.shape[1]
    experts_all = router_weight.shape[1]
    exp_here = experts_all // seq_count
    capacity = max(2, 2 * quarter * TOPK // experts_all)
    quarter_units = FF // tensor_parallel_count
    heads_here = QUERY_HEADS // tensor_parallel_count
    key_value_local = KEY_VALUE_HEADS // tensor_parallel_count
    prompt_rows = lax.all_gather(hidden_in, "tp", axis=0, tiled=True)
    column_span = prompt_rows.shape[0]
    normed = rms_scale(prompt_rows.astype(jnp.float32), attention_gain).astype(jnp.bfloat16)
    trainer_rows = attention_trainer_copy.shape[0]
    query_cols = attention_trainer_copy[:, : QUERY_HEADS * HEAD_SIZE].reshape(
        trainer_rows, tensor_parallel_count, heads_here * HEAD_SIZE
    )
    key_columns = attention_trainer_copy[
        :, QUERY_HEADS * HEAD_SIZE : (QUERY_HEADS + KEY_VALUE_HEADS) * HEAD_SIZE
    ].reshape(trainer_rows, tensor_parallel_count, key_value_local * HEAD_SIZE)
    value_columns = attention_trainer_copy[
        :, (QUERY_HEADS + KEY_VALUE_HEADS) * HEAD_SIZE :
    ].reshape(trainer_rows, tensor_parallel_count, key_value_local * HEAD_SIZE)
    joined = (
        jnp.concatenate([query_cols, key_columns, value_columns], axis=2)
        .reshape(trainer_rows, -1)
        .astype(jnp.bfloat16)
    )
    head_rows = lax.all_to_all(joined, "tp", split_axis=1, concat_axis=0, tiled=True)
    projected_rows = jnp.dot(
        normed,
        lax.all_gather(head_rows, "seq", axis=0, tiled=True),
        preferred_element_type=jnp.float32,
    )
    positions = jnp.arange(column_span)
    query_rows = projected_rows[:, : heads_here * HEAD_SIZE].reshape(
        column_span, heads_here, HEAD_SIZE
    )
    keys_raw = projected_rows[
        :, heads_here * HEAD_SIZE : (heads_here + key_value_local) * HEAD_SIZE
    ].reshape(column_span, key_value_local, HEAD_SIZE)
    values_local_rows = (
        projected_rows[:, (heads_here + key_value_local) * HEAD_SIZE :]
        .reshape(column_span, key_value_local, HEAD_SIZE)
        .astype(jnp.bfloat16)
    )
    query_rows = rotate(rms_scale(query_rows, query_gain), positions).astype(jnp.bfloat16)
    keys_rotated = rotate(rms_scale(keys_raw, key_gain), positions).astype(jnp.bfloat16)
    prompt_length = lengths[0]
    context_rows = attend_prompt(
        query_rows.reshape(column_span, key_value_local, QUERY_HEADS // KEY_VALUE_HEADS, HEAD_SIZE),
        keys_rotated,
        values_local_rows,
        prompt_length,
    )
    attention_sums = lax.psum_scatter(
        jnp.dot(context_rows, output_proj, preferred_element_type=jnp.float32).astype(jnp.bfloat16),
        "tp",
        scatter_dimension=0,
        tiled=True,
    ).astype(jnp.float32)
    after_attn = hidden_in.astype(jnp.float32) + attention_sums
    mixed = rms_scale(after_attn, post_gain).astype(jnp.bfloat16)
    logits = jnp.dot(mixed, router_weight, preferred_element_type=jnp.float32)
    chosen = jnp.take_along_axis(logits, routes, axis=1)
    raised = jnp.exp(chosen)
    gates = raised / jnp.sum(raised, axis=1, keepdims=True)
    pair_expert = routes.reshape(-1)
    hits = (pair_expert[:, None] == jnp.arange(experts_all, dtype=jnp.int32)[None, :]).astype(
        jnp.int32
    )
    before = jnp.cumsum(hits, axis=0) - hits
    slot_index = jnp.sum(before * hits, axis=1)
    target = pair_expert * capacity + slot_index
    mixed_order = regroup(mixed, seq_count, tensor_parallel_count)
    outgoing = (
        jnp.zeros((experts_all * capacity, width), jnp.bfloat16)
        .at[target]
        .set(jnp.repeat(mixed_order, TOPK, axis=0))
    )
    outgoing = outgoing.reshape(seq_count, exp_here, capacity, width)
    incoming = lax.all_to_all(outgoing, "seq", split_axis=0, concat_axis=0, tiled=True)
    by_expert = lax.all_to_all(
        gate_up_master.astype(jnp.bfloat16), "seq", split_axis=0, concat_axis=1, tiled=True
    )
    full_gate_up, full_down = (
        lax.all_gather(by_expert, "tp", axis=1, tiled=True),
        lax.all_gather(down_weight, "tp", axis=1, tiled=True),
    )
    results = []
    for expert_slot in range(exp_here):
        flat_rows = incoming[:, expert_slot].reshape(-1, width)
        both = jnp.dot(flat_rows, full_gate_up[expert_slot], preferred_element_type=jnp.float32)
        units = (jax.nn.silu(both[:, :FF]) * both[:, FF:]).astype(jnp.bfloat16)
        summed = jnp.zeros((flat_rows.shape[0], width), jnp.float32)
        for block_index in range(tensor_parallel_count):
            lower = block_index * quarter_units
            produced = jnp.dot(
                units[:, lower : lower + quarter_units],
                full_down[expert_slot, lower : lower + quarter_units],
                preferred_element_type=jnp.float32,
            )
            summed = summed + lax.optimization_barrier(produced.astype(jnp.bfloat16)).astype(
                jnp.float32
            )
        results.append(summed.astype(jnp.bfloat16).reshape(seq_count, capacity, width))
    expert_result = jnp.stack(results, axis=1)
    returned = lax.all_to_all(expert_result, "seq", split_axis=0, concat_axis=0, tiled=True)
    pair_out = returned.reshape(experts_all * capacity, width)[target]
    combined = jnp.sum(
        gates[:, :, None] * pair_out.reshape(quarter, TOPK, width).astype(jnp.float32), axis=1
    )
    own_places = tp_place * quarter + jnp.arange(quarter)
    live_rows = own_places < prompt_length
    hidden_leaving = jnp.where(live_rows[:, None], after_attn + combined, 0.0).astype(jnp.bfloat16)
    live = (positions < prompt_length)[:, None, None]
    zero_value = jnp.zeros((), jnp.bfloat16)
    keys_kept = jnp.where(live, keys_rotated, zero_value)
    values_kept = jnp.where(live, values_local_rows, zero_value)
    pages_here = column_span // PAGE_POSITIONS
    prompt_pages = jnp.stack([keys_kept, values_kept], axis=1)
    prompt_pages = prompt_pages.reshape(
        pages_here, PAGE_POSITIONS, 2, key_value_local, HEAD_SIZE
    ).transpose(0, 2, 3, 1, 4)
    paged_cache = jnp.zeros(
        (2 * pages_here, 2, key_value_local, PAGE_POSITIONS, HEAD_SIZE), jnp.bfloat16
    )
    paged_cache = paged_cache.at[page_table[0]].set(prompt_pages)
    return (hidden_leaving, paged_cache)


def solution(mesh):
    return jax.shard_map(
        on_device,
        mesh=mesh,
        in_specs=(
            P(("seq", "tp"), None),
            P(),
            P(("seq", "tp"), None),
            P(),
            P(),
            P("tp", None),
            P(),
            P(),
            P(None, ("seq", "tp"), None),
            P("seq", "tp", None),
            P(("seq", "tp"), None),
            P("seq"),
            P("seq", None),
        ),
        out_specs=(P(("seq", "tp"), None), P("seq", None, "tp", None, None)),
        check_vma=False,
    )
```

profile of v0, /device:TPU:0, one launch (start us, length us, event | category | flops | bytes accessed | tf_op | source)
XLA Modules:
  0.0 576.1 jit_solution(6042989574184190259)
XLA Ops:
  8.0 1.4 convert.33
  10.2 37.1 %all_to_all.44 = bf16[64,4,1280]{2,0,1:T(8,128)(2,1)} all-to-all(bf16[64,4,1280]{2,0,1:T(8,128)(2,1)S(1)} %copy.84), channel_id=1, replica_groups=mesh['seq'=8,'tp'=4] {'tp'}, dimensions={1} | all-to-all | bytes 1310720 | tf_op jit(solution)/shard_map/all_to_all | solution.py:103
  47.4 4.9 convert_element_type.164
  52.3 3.9 all-to-all-start.2
  58.8 1.6 fusion.3
  60.4 55.7 %all-gather.7.cloned.1.call-done = bf16[2048,1280]{1,0:T(8,128)(2,1)} async-done(((bf16[256,1280]{1,0:T(8,128)(2,1)}), bf16[2048,1280]{1,0:T(8,128)(2,1)}) %all-gather.7.cloned.1.call-update) | async-done | bytes 5242896 | tf_op jit(solution)/shard_map/all_gather | solution.py:106
  116.1 4.4 fusion.12
  120.7 1.3 slice_bitcast_fusion.5
  122.1 1.2 fusion.38
  123.9 1.6 fusion.14
  127.2 1.7 convolution_convert_fusion.9
  129.5 2.3 convolution_convert_fusion.8
  131.8 2.0 copy.97
  136.5 19.9 %reduce-scatter.2.cloned.1.call-done = bf16[64,2048]{1,0:T(8,128)(2,1)} async-done(((bf16[256,2048]{1,0:T(8,128)(2,1)}), bf16[64,2048]{1,0:T(8,128)(2,1)}) %reduce-scatter.2.cloned.1.call-update) | async-done | bytes 262160 | tf_op jit(solution)/shard_map/reduce_scatter | solution.py:130
  159.7 6.4 %scatter_custom_fusion = bf16[1024,2048]{1,0:T(8,128)(2,1)} fusion(s32[512]{0:T(512)S(1)} %bitcast.172, bf16[]{:T(256)} %constant.66.clone.1, bf16[64,2048]{1,0:T(8,128)(2,1)S(1)} %reshape.412), kind=kCustom, calls=%fused_computation.28 | custom fusion | bytes 4456450 | tf_op jit(solution)/shard_map/scatter | solution.py:153
  166.1 52.7 %all_to_all.45 = bf16[8,2,64,2048]{3,2,1,0:T(8,128)(2,1)S(1)} all-to-all(bf16[8,2,64,2048]{3,2,1,0:T(8,128)(2,1)} %bitcast.156), channel_id=1, replica_groups=mesh['seq'=8,'tp'=4] {'seq'}, dimensions={0} | all-to-all | bytes 8388608 | tf_op jit(solution)/shard_map/all_to_all | solution.py:156
  218.8 2.5 fusion.53
  221.3 153.5 %all-gather.9.cloned.1.call-done = bf16[2,2048,1536]{2,1,0:T(8,128)(2,1)} async-done(((bf16[2,512,1536]{2,1,0:T(8,128)(2,1)}), bf16[2,2048,1536]{2,1,0:T(8,128)(2,1)}) %all-gather.9.cloned.1.call-update) | async-done | bytes 12582928 | tf_op jit(solution)/shard_map/all_gather | solution.py:161
  374.8 6.5 %fusion.1 = f32[512,1536]{1,0:T(8,128)S(1)} fusion(bf16[512,2048]{1,0:T(8,128)(2,1)} %bitcast.165, bf16[2,2048,1536]{2,1,0:T(8,128)(2,1)} %all-gather.9.cloned.1.call-done), kind=kOutput, calls=%fused_computation.7 | convolution fusion | flops 3221225472 | bytes 11534336 | tf_op jit(solution)/shard_map/dot_general | solution.py:167
  383.4 3.4 fusion
  387.3 102.6 %all-gather.11.cloned.1.call-done = bf16[2,768,2048]{2,1,0:T(8,128)(2,1)} async-done(((bf16[2,192,2048]{2,1,0:T(8,128)(2,1)}), bf16[2,768,2048]{2,1,0:T(8,128)(2,1)}) %all-gather.11.cloned.1.call-update) | async-done | bytes 6291472 | tf_op jit(solution)/shard_map/all_gather | solution.py:162
  489.9 2.0 convolution_convert_fusion
  491.9 1.8 convolution_convert_fusion.1
  493.8 1.9 convolution_convert_fusion.2
  499.4 2.0 add_convert_fusion
  501.3 2.0 add_convert_fusion.1
  503.3 2.6 pad_maximum_fusion
  505.9 4.7 all-to-all-start.3
  512.9 3.9 gather_fusion.1
  517.1 42.6 %all-to-all-done.3 = bf16[8,2,64,2048]{3,2,1,0:T(8,128)(2,1)} async-done(((bf16[8,2,64,2048]{3,2,1,0:T(8,128)(2,1)}), bf16[8,2,64,2048]{3,2,1,0:T(8,128)(2,1)}, u32[]{:S(2)}, u32[]{:S(2)}) %all-to-all-start.3) | async-done | bytes 4194336 | tf_op jit(solution)/shard_map/all_to_all | solution.py:182
  559.7 7.1 %gather_fusion = bf16[512,2048]{1,0:T(8,128)(2,1)S(1)} fusion(bf16[1024,2048]{1,0:T(8,128)(2,1)} %bitcast.40, s32[1024]{0:T(1024)S(1)} %pad_clamp_fusion), kind=kCustom, calls=%fused_computation | custom fusion | bytes 4196352 | tf_op jit(solution)/shard_map/gather | solution.py:183
  566.9 1.8 fusion.2
  (117 shorter events, 22.0 us)
Async XLA Ops:
  7.2 505.6 %copy-start = (bf16[2048,16]{0,1:T(8,128)(2,1)S(1)}, bf16[2048,16]{0,1:T(8,128)(2,1)}, u32[]{:S(2)}) copy-start(bf16[2048,16]{0,1:T(8,128)(2,1)} %param.20) | copy-start | bytes 196612
  7.2 51.6 %all-gather.5.cloned.1.call-start = ((), (), s32[]{:S(2)}) async-start(), calls=%async_computation.5 | async-start | bytes 1310720 | tf_op jit(solution)/shard_map/all_gather | solution.py:85
  7.9 108.2 %all-gather.7.cloned.1.call-start = ((), (), s32[]{:S(2)}) async-start(), calls=%async_computation.6 | async-start | bytes 5898240 | tf_op jit(solution)/shard_map/all_gather | solution.py:106
  52.3 63.9 %copy-start.17 = (f32[2048]{0:T(1024)S(1)}, f32[2048]{0:T(1024)}, u32[]{:S(2)}) copy-start(f32[2048]{0:T(1024)} %param.14) | copy-start | bytes 24580
  52.3 79.5 %all-to-all-start.2 = ((bf16[16,64,1536]{2,1,0:T(8,128)(2,1)}), bf16[16,64,1536]{2,1,0:T(8,128)(2,1)S(1)}, u32[]{:S(2)}, u32[]{:S(2)}) async-start(bf16[16,64,1536]{2,1,0:T(8,128)(2,1)} %convert_element_type.164), calls=%async_computation.3 | async-start | bytes 6291456 | tf_op jit(solution)/shard_map/all_to_all | solution.py:157
  56.1 100.3 %reduce-scatter.2.cloned.1.call-start = ((), (), s32[]{:S(2)}) async-start(), calls=%async_computation.7 | async-start | bytes 1310720 | tf_op jit(solution)/shard_map/reduce_scatter | solution.py:130
  120.5 3.0 copy-start.5
  120.5 1.4 copy-start.13
  121.9 2.0 copy-start.14
  123.9 1.7 copy-start.7
  125.5 0.8 copy-start.8
  125.5 0.9 copy-start.11
  127.2 2.3 copy-start.16
  131.8 243.1 %all-gather.9.cloned.1.call-start = ((), (), s32[]{:S(2)}) async-start(), calls=%async_computation.8 | async-start | bytes 15728640 | tf_op jit(solution)/shard_map/all_gather | solution.py:161
  133.8 0.7 copy-start.10
  133.8 22.6 %copy-start.2 = (bf16[64,2048]{1,0:T(8,128)(2,1)S(1)}, bf16[64,2048]{1,0:T(8,128)(2,1)}, u32[]{:S(2)}) copy-start(bf16[64,2048]{1,0:T(8,128)(2,1)} %param.13) | copy-start | bytes 786436
  133.8 23.8 %copy-start.12 = (f32[2048]{0:T(1024)S(1)}, f32[2048]{0:T(1024)}, u32[]{:S(2)}) copy-start(f32[2048]{0:T(1024)} %param.19) | copy-start | bytes 24580
  133.8 356.1 %all-gather.11.cloned.1.call-start = ((), (), s32[]{:S(2)}) async-start(), calls=%async_computation.9 | async-start | bytes 7864320 | tf_op jit(solution)/shard_map/all_gather | solution.py:162
  374.8 7.4 %copy-start.15 = (bf16[2,2048,1536]{2,1,0:T(8,128)(2,1)S(1)}, bf16[2,2048,1536]{2,1,0:T(8,128)(2,1)}, u32[]{:S(2)}) copy-start(bf16[2,2048,1536]{2,1,0:T(8,128)(2,1)} %all-gather.9.cloned.1.call-done) | copy-start | bytes 37748740
  381.3 2.1 copy-start.4
  489.9 5.8 %copy-start.1 = (bf16[2,768,2048]{2,1,0:T(8,128)(2,1)S(1)}, bf16[2,768,2048]{2,1,0:T(8,128)(2,1)}, u32[]{:S(2)}) copy-start(bf16[2,768,2048]{2,1,0:T(8,128)(2,1)} %all-gather.11.cloned.1.call-done) | copy-start | bytes 18874372
  505.9 4.9 copy-start.18
  505.9 4.9 copy-start.9
  505.9 53.8 %all-to-all-start.3 = ((bf16[8,2,64,2048]{3,2,1,0:T(8,128)(2,1)}), bf16[8,2,64,2048]{3,2,1,0:T(8,128)(2,1)}, u32[]{:S(2)}, u32[]{:S(2)}) async-start(bf16[8,2,64,2048]{3,2,1,0:T(8,128)(2,1)} %pad_maximum_fusion), calls=%async_computation.4 | async-start | bytes 8388608 | tf_op jit(solution)/shard_map/all_to_all | solution.py:182
  512.7 4.1 copy-start.6
  566.9 1.9 copy-start.3
Sparse Core Ops, SparseCore 0:
  9.6 41.2 all-gather.4
  52.8 63.3 all-gather.6
  131.9 24.5 reduce-scatter.1
  157.9 216.8 all-gather.8
  376.3 113.5 all-gather.10
where the time goes:
time: 577 us; the launch traced here: 576 us
  waiting for transfers between devices  375 us (65%)
  blocking collectives  89.9 us (16%)
  local copies, waits for them, and re-layouts  29.4 us (5%)
  other arithmetic  28.8 us (5%)
  matrix products  28.7 us (5%)
  between operations  15 us (3%)
  starting transfers between devices  8.91 us (2%)
    all_gather x1, waiting for transfers between devices, on_device(): lax.all_gather(by_expert, 'tp', axis=1, tiled=True)  153 us
    all_gather x1, waiting for transfers between devices, on_device(): lax.all_gather(down_weight, 'tp', axis=1, tiled=True)  103 us
    all_gather x1, waiting for transfers between devices, on_device(): lax.all_gather(head_rows, 'seq', axis=0, tiled=True)  55.7 us
    all_to_all x1, blocking collectives, on_device(): lax.all_to_all(outgoing, 'seq', split_axis=0, concat_axis=0, tiled=True)  52.7 us
    all_to_all x1, waiting for transfers between devices, on_device(): lax.all_to_all(expert_result, 'seq', split_axis=0, concat_axis=0, tiled=T...  42.6 us
    all_to_all x1, blocking collectives, on_device(): lax.all_to_all(joined, 'tp', split_axis=1, concat_axis=0, tiled=True)  37.1 us
    reduce_scatter x1, waiting for transfers between devices, on_device(): lax.psum_scatter(jnp.dot(context_rows, output_proj, preferred_element_typ...  19.9 us
  transfers between devices with their start and end apart: 7, of which 5 were waited for; matrix products, arithmetic and copies ran while one was open for 10% of the time, Pallas kernels for 0%

commit v1 on v0

--- a/solution.py
+++ b/solution.py
@@ -3,7 +3,7 @@
 import jax
 import jax.numpy as jnp
 from jax import lax
-from jax.sharding import PartitionSpec as P
+from jax.sharding import Mesh, PartitionSpec as P
 
 QUERY_HEADS = 32
 KEY_VALUE_HEADS = 4
@@ -50,13 +50,18 @@
     return context_rows.astype(jnp.bfloat16).reshape(column_span, -1)
 
 
+def name_experts(routes, experts_all):
+    experts = jnp.arange(experts_all, dtype=jnp.int32)
+    return jnp.any(routes[:, :, None] == experts[None, None, :], axis=1)
+
+
 def regroup(features, seq_count, tensor_parallel_count):
     leading = features.shape[:-1]
     blocks = features.reshape(leading + (seq_count, tensor_parallel_count, -1))
     return jnp.swapaxes(blocks, -3, -2).reshape(leading + (-1,))
 
 
-def on_device(
+def on_device_dispatch(
     hidden_in,
     attention_gain,
     attention_trainer_copy,
@@ -136,21 +141,20 @@
     after_attn = hidden_in.astype(jnp.float32) + attention_sums
     mixed = rms_scale(after_attn, post_gain).astype(jnp.bfloat16)
     logits = jnp.dot(mixed, router_weight, preferred_element_type=jnp.float32)
-    chosen = jnp.take_along_axis(logits, routes, axis=1)
-    raised = jnp.exp(chosen)
+    hits = name_experts(routes, experts_all)
+    raised = jnp.where(hits, jnp.exp(logits), 0.0)
     gates = raised / jnp.sum(raised, axis=1, keepdims=True)
-    pair_expert = routes.reshape(-1)
-    hits = (pair_expert[:, None] == jnp.arange(experts_all, dtype=jnp.int32)[None, :]).astype(
-        jnp.int32
-    )
-    before = jnp.cumsum(hits, axis=0) - hits
-    slot_index = jnp.sum(before * hits, axis=1)
-    target = pair_expert * capacity + slot_index
+    row = jnp.arange(quarter)
+    earlier = (row[None, :] < row[:, None]).astype(jnp.bfloat16)
+    before = jnp.dot(earlier, hits.astype(jnp.bfloat16), preferred_element_type=jnp.float32)
+    before = before.astype(jnp.int32)
+    slots = jnp.arange(capacity, dtype=jnp.int32)
+    placed = hits[:, :, None] & (before[:, :, None] == slots[None, None, :])
+    placed_gates = jnp.where(placed, gates[:, :, None], 0.0).reshape(quarter, -1)
+    placed = placed.reshape(quarter, -1).astype(jnp.bfloat16)
     mixed_order = regroup(mixed, seq_count, tensor_parallel_count)
-    outgoing = (
-        jnp.zeros((experts_all * capacity, width), jnp.bfloat16)
-        .at[target]
-        .set(jnp.repeat(mixed_order, TOPK, axis=0))
+    outgoing = jnp.dot(placed.T, mixed_order, preferred_element_type=jnp.float32).astype(
+        jnp.bfloat16
     )
     outgoing = outgoing.reshape(seq_count, exp_here, capacity, width)
     incoming = lax.all_to_all(outgoing, "seq", split_axis=0, concat_axis=0, tiled=True)
@@ -180,48 +184,202 @@
         results.append(summed.astype(jnp.bfloat16).reshape(seq_count, capacity, width))
     expert_result = jnp.stack(results, axis=1)
     returned = lax.all_to_all(expert_result, "seq", split_axis=0, concat_axis=0, tiled=True)
-    pair_out = returned.reshape(experts_all * capacity, width)[target]
-    combined = jnp.sum(
-        gates[:, :, None] * pair_out.reshape(quarter, TOPK, width).astype(jnp.float32), axis=1
+    combined = jnp.dot(
+        placed_gates,
+        returned.reshape(experts_all * capacity, width).astype(jnp.float32),
+        precision=lax.Precision.HIGHEST,
     )
     own_places = tp_place * quarter + jnp.arange(quarter)
     live_rows = own_places < prompt_length
     hidden_leaving = jnp.where(live_rows[:, None], after_attn + combined, 0.0).astype(jnp.bfloat16)
-    live = (positions < prompt_length)[:, None, None]
+    return (hidden_leaving, fill_cache(keys_rotated, values_local_rows, prompt_length, page_table))
+
+
+PLANE = ("chip", "core")
+EVERY = ("chip", "core", "tp")
+ROWS = ("chip", "tp")
+DENSE_BYTES = 16 << 20
+
+
+def project_and_attend(
+    hidden_in, attention_gain, attention_trainer_copy, query_gain, key_gain, prompt_length
+):
+    tensor_parallel_count = lax.axis_size("tp")
+    heads_here = QUERY_HEADS // tensor_parallel_count
+    key_value_local = KEY_VALUE_HEADS // tensor_parallel_count
+    prompt_rows = lax.all_gather(hidden_in, "tp", axis=0, tiled=True)
+    column_span = prompt_rows.shape[0]
+    normed = rms_scale(prompt_rows.astype(jnp.float32), attention_gain).astype(jnp.bfloat16)
+    trainer_rows = attention_trainer_copy.shape[0]
+    query_end = QUERY_HEADS * HEAD_SIZE
+    key_end = query_end + KEY_VALUE_HEADS * HEAD_SIZE
+    rounded = attention_trainer_copy.astype(jnp.bfloat16)
+    parts = [
+        part.reshape(trainer_rows, tensor_parallel_count, -1)
+        for part in (rounded[:, :query_end], rounded[:, query_end:key_end], rounded[:, key_end:])
+    ]
+    joined = jnp.concatenate(parts, axis=2).reshape(trainer_rows, -1)
+    head_rows = lax.all_to_all(joined, "tp", split_axis=1, concat_axis=0, tiled=True)
+    projected_rows = jnp.dot(
+        normed,
+        lax.all_gather(head_rows, PLANE, axis=0, tiled=True),
+        preferred_element_type=jnp.float32,
+    )
+    positions = jnp.arange(column_span)
+    query_rows = projected_rows[:, : heads_here * HEAD_SIZE].reshape(
+        column_span, heads_here, HEAD_SIZE
+    )
+    keys_raw = projected_rows[
+        :, heads_here * HEAD_SIZE : (heads_here + key_value_local) * HEAD_SIZE
+    ].reshape(column_span, key_value_local, HEAD_SIZE)
+    values_rows = (
+        projected_rows[:, (heads_here + key_value_local) * HEAD_SIZE :]
+        .reshape(column_span, key_value_local, HEAD_SIZE)
+        .astype(jnp.bfloat16)
+    )
+    query_rows = rotate(rms_scale(query_rows, query_gain), positions).astype(jnp.bfloat16)
+    keys_rotated = rotate(rms_scale(keys_raw, key_gain), positions).astype(jnp.bfloat16)
+    context_rows = attend_prompt(
+        query_rows.reshape(column_span, key_value_local, QUERY_HEADS // KEY_VALUE_HEADS, HEAD_SIZE),
+        keys_rotated,
+        values_rows,
+        prompt_length,
+    )
+    return context_rows, keys_rotated, values_rows
+
+
+def fill_cache(keys_rotated, values_rows, prompt_length, page_table):
+    column_span, key_value_local, _ = keys_rotated.shape
+    live = (jnp.arange(column_span) < prompt_length)[:, None, None]
     zero_value = jnp.zeros((), jnp.bfloat16)
     keys_kept = jnp.where(live, keys_rotated, zero_value)
-    values_kept = jnp.where(live, values_local_rows, zero_value)
+    values_kept = jnp.where(live, values_rows, zero_value)
     pages_here = column_span // PAGE_POSITIONS
     prompt_pages = jnp.stack([keys_kept, values_kept], axis=1)
     prompt_pages = prompt_pages.reshape(
         pages_here, PAGE_POSITIONS, 2, key_value_local, HEAD_SIZE
     ).transpose(0, 2, 3, 1, 4)
-    paged_cache = jnp.zeros(
-        (2 * pages_here, 2, key_value_local, PAGE_POSITIONS, HEAD_SIZE), jnp.bfloat16
-    )
-    paged_cache = paged_cache.at[page_table[0]].set(prompt_pages)
-    return (hidden_leaving, paged_cache)
+    slots = jnp.arange(2 * pages_here, dtype=jnp.int32)[:, None, None, None, None]
+    paged_cache = jnp.zeros((2 * pages_here,) + prompt_pages.shape[1:], jnp.bfloat16)
+    for page in range(pages_here):
+        paged_cache = jnp.where(slots == page_table[0, page], prompt_pages[page][None], paged_cache)
+    return paged_cache
+
+
+def on_device(
+    hidden_in,
+    attention_gain,
+    attention_trainer_copy,
+    query_gain,
+    key_gain,
+    output_proj,
+    post_gain,
+    router_weight,
+    gate_up_master,
+    down_weight,
+    routes,
+    lengths,
+    page_table,
+):
+    tensor_parallel_count = lax.axis_size("tp")
+    seq_count = lax.axis_size("chip") * lax.axis_size("core")
+    tp_place = lax.axis_index("tp")
+    chip_place = lax.axis_index("chip")
+    quarter, width = hidden_in.shape
+    experts_all = router_weight.shape[1]
+    exp_here = experts_all // seq_count
+    units_here = FF // tensor_parallel_count
+    prompt_length = lengths[0]
+    master_rows = gate_up_master.shape[1]
+    blocks = (
+        gate_up_master.astype(jnp.bfloat16)
+        .reshape(seq_count, exp_here, master_rows, 2, tensor_parallel_count, units_here)
+        .transpose(0, 4, 2, 3, 1, 5)
+        .reshape(seq_count * tensor_parallel_count, master_rows, 2 * exp_here * units_here)
+    )
+    mine = lax.all_to_all(blocks, EVERY, split_axis=0, concat_axis=0, tiled=True)
+    mine = mine.reshape(-1, 2 * exp_here * units_here)
+    pair_gate_up = lax.all_gather(mine, "core", axis=0)
+    pair_down = lax.all_gather(down_weight.reshape(-1, width), "core", axis=0)
+    pair_routes = lax.all_gather(routes, ROWS, axis=0, tiled=True)
+
+    context_rows, keys_rotated, values_rows = project_and_attend(
+        hidden_in, attention_gain, attention_trainer_copy, query_gain, key_gain, prompt_length
+    )
+    attention_sums = lax.psum_scatter(
+        jnp.dot(context_rows, output_proj, preferred_element_type=jnp.float32).astype(jnp.bfloat16),
+        "tp",
+        scatter_dimension=0,
+        tiled=True,
+    ).astype(jnp.float32)
+    after_attn = hidden_in.astype(jnp.float32) + attention_sums
+    mixed = rms_scale(after_attn, post_gain).astype(jnp.bfloat16)
+    group_rows = lax.all_gather(mixed, "tp", axis=0, tiled=False)
+    group_rows = lax.all_gather(group_rows, "chip", axis=0, tiled=True).reshape(-1, width)
+
+    logits = jnp.dot(group_rows, router_weight, preferred_element_type=jnp.float32)
+    named = name_experts(pair_routes, experts_all)
+    raised = jnp.where(named, jnp.exp(logits), 0.0)
+    gates = raised / jnp.sum(raised, axis=1, keepdims=True)
+    chip_gates = lax.dynamic_slice_in_dim(gates, chip_place * 2 * exp_here, 2 * exp_here, axis=1)
+    column_expert = jnp.arange(exp_here * units_here) // units_here
+    halves = []
+    for core in range(2):
+        both = jnp.dot(group_rows, pair_gate_up[core], preferred_element_type=jnp.float32)
+        spread = jnp.zeros((group_rows.shape[0], exp_here * units_here), jnp.float32)
+        for slot in range(exp_here):
+            gate = chip_gates[:, core * exp_here + slot][:, None]
+            spread = jnp.where(column_expert[None, :] == slot, gate, spread)
+        hidden_units = exp_here * units_here
+        units = jax.nn.silu(both[:, :hidden_units]) * both[:, hidden_units:] * spread
+        halves.append(units.astype(jnp.bfloat16))
+    partial = jnp.dot(
+        jnp.concatenate(halves, axis=1),
+        pair_down.reshape(-1, width),
+        preferred_element_type=jnp.float32,
+    ).astype(jnp.bfloat16)
+    combined = lax.psum_scatter(partial, "chip", scatter_dimension=0, tiled=True)
+    combined = lax.psum_scatter(combined, "tp", scatter_dimension=0, tiled=True)
+    own_places = tp_place * quarter + jnp.arange(quarter)
+    live_rows = own_places < prompt_length
+    hidden_leaving = jnp.where(
+        live_rows[:, None], after_attn + combined.astype(jnp.float32), 0.0
+    ).astype(jnp.bfloat16)
+    return (hidden_leaving, fill_cache(keys_rotated, values_rows, prompt_length, page_table))
+
+
+def specs(seq):
+    rows = P(seq + ("tp",), None)
+    return dict(
+        in_specs=(
+            rows,
+            P(),
+            rows,
+            P(),
+            P(),
+            P("tp", None),
+            P(),
+            P(),
+            P(None, seq + ("tp",), None),
+            P(seq, "tp", None),
+            rows,
+            P(seq),
+            P(seq, None),
+        ),
+        out_specs=(rows, P(seq, None, "tp", None, None)),
+        check_vma=False,
+    )
 
 
 def solution(mesh):
-    return jax.shard_map(
-        on_device,
-        mesh=mesh,
-        in_specs=(
-            P(("seq", "tp"), None),
-            P(),
-            P(("seq", "tp"), None),
-            P(),
-            P(),
-            P("tp", None),
-            P(),
-            P(),
-            P(None, ("seq", "tp"), None),
-            P("seq", "tp", None),
-            P(("seq", "tp"), None),
-            P("seq"),
-            P("seq", None),
-        ),
-        out_specs=(P(("seq", "tp"), None), P("seq", None, "tp", None, None)),
-        check_vma=False,
-    )
+    seq_count, tensor_parallel_count = mesh.shape["seq"], mesh.shape["tp"]
+    cores = Mesh(mesh.devices.reshape(seq_count // 2, 2, tensor_parallel_count), EVERY)
+
+    def layer(hidden_in, *others):
+        if hidden_in.size * hidden_in.dtype.itemsize <= DENSE_BYTES:
+            run = jax.shard_map(on_device, mesh=cores, **specs(PLANE))
+        else:
+            run = jax.shard_map(on_device_dispatch, mesh=mesh, **specs(("seq",)))
+        return run(hidden_in, *others)
+
+    return layer

time: 577 us -> 415 us (0.72)
  waiting for transfers between devices: 375 us -> 174 us
  blocking collectives: 89.9 us -> 151 us
  other arithmetic: 28.8 us -> 18.8 us
  starting transfers between devices: 8.91 us -> 0.54 us
    all_gather x4 -> x6, waiting for transfers between devices: 312 us -> 69.5 us  [the longest x1 40.6 us: project_and_attend(): lax.all_gather(head_rows, PLANE, axis=0, tiled=True)]
    reduce_scatter x0 -> x2, waiting for transfers between devices: none -> 75.5 us  [the longest x1 50.1 us: on_device(): lax.psum_scatter(partial, 'chip', scatter_dimension=0, tiled=True)]
    all_to_all x2 -> x0, waiting for transfers between devices: 42.6 us -> none  [the longest x1 42.6 us: on_device(): lax.all_to_all(expert_result, 'seq', split_axis=0, concat_axis=0, tiled=T...]
    all_gather x0 -> x1, blocking collectives: none -> 40.2 us  [on_device(): pair_routes = lax.all_gather(routes, ROWS, axis=0, tiled=True)]
    reshape x6, local copies, waits for them, and re-layouts: 1.47 us -> 23.4 us  [the longest x3 23 us: on_device(): blocks = gate_up_master.astype(jnp.bfloat16).reshape(seq_count, exp_here,...]
    all_to_all x2, blocking collectives: 89.9 us -> 111 us  [the longest x1 74.1 us: on_device(): lax.all_to_all(blocks, EVERY, split_axis=0, concat_axis=0, tiled=True)]
    gather x6 -> x0, local copies, waits for them, and re-layouts: 11.4 us -> none  [the longest x1 7.13 us: on_device(): pair_out = returned.reshape(experts_all * capacity, width)[target]]
    all_to_all x2 -> x0, starting transfers between devices: 8.53 us -> none  [the longest x1 4.67 us: on_device(): lax.all_to_all(expert_result, 'seq', split_axis=0, concat_axis=0, tiled=T...]
  transfers between devices with their start and end apart: 7 -> 9, of which waited for: 5 -> 6; matrix products, arithmetic and copies ran while one was open for 10% -> 12% of each run, Pallas kernels for 0% -> 0%
where the time goes in v1:
time: 415 us; the launch traced here: 414 us
  waiting for transfers between devices  174 us (42%)
  blocking collectives  151 us (36%)
  matrix products  28.4 us (7%)
  local copies, waits for them, and re-layouts  26.4 us (6%)
  other arithmetic  18.8 us (5%)
  between operations  15 us (4%)
    all_to_all x1, blocking collectives, on_device(): lax.all_to_all(blocks, EVERY, split_axis=0, concat_axis=0, tiled=True)  74.1 us
    reduce_scatter x1, waiting for transfers between devices, on_device(): lax.psum_scatter(partial, 'chip', scatter_dimension=0, tiled=True)  50.1 us
    all_gather x1, waiting for transfers between devices, project_and_attend(): lax.all_gather(head_rows, PLANE, axis=0, tiled=True)  40.6 us
    all_gather x1, blocking collectives, on_device(): pair_routes = lax.all_gather(routes, ROWS, axis=0, tiled=True)  40.2 us
    all_to_all x1, blocking collectives, project_and_attend(): lax.all_to_all(joined, 'tp', split_axis=1, concat_axis=0, tiled=True)  37.1 us
    reduce_scatter x1, waiting for transfers between devices, on_device(): lax.psum_scatter(jnp.dot(context_rows, output_proj, preferred_element_typ...  27.2 us
    all_gather x1, waiting for transfers between devices, on_device(): group_rows = lax.all_gather(mixed, 'tp', axis=0, tiled=False)  26.7 us
    reduce_scatter x1, waiting for transfers between devices, on_device(): combined = lax.psum_scatter(combined, 'tp', scatter_dimension=0, tiled=True)  25.5 us
  transfers between devices with their start and end apart: 9, of which 6 were waited for; matrix products, arithmetic and copies ran while one was open for 12% of the time, Pallas kernels for 0%

profile of v1, /device:TPU:0, one launch (start us, length us, event | category | flops | bytes accessed | tf_op | source)
XLA Modules:
  0.0 414.4 jit_solution(6719994422951849404)
XLA Ops:
  7.2 0.7 all-gather.9.cloned.1.call-update
  8.0 1.4 convert_element_type.94
  10.3 37.1 %all_to_all.21 = bf16[64,4,1280]{2,0,1:T(8,128)(2,1)} all-to-all(bf16[64,4,1280]{2,0,1:T(8,128)(2,1)S(1)} %copy.46), channel_id=1, replica_groups=mesh['chip'=4,'core'=2,'tp'=4] {'tp'}, dimensions={1} | all-to-all | bytes 1310720 | tf_op jit(solution)/shard_map/all_to_all | solution.py:222
  48.8 2.1 all-gather.9.cloned.1.call-done
  50.9 1.5 fusion.2
  52.4 40.6 %all-gather.11.cloned.1.call-done = bf16[2048,1280]{1,0:T(8,128)(2,1)} async-done(((bf16[256,1280]{1,0:T(8,128)(2,1)}), bf16[2048,1280]{1,0:T(8,128)(2,1)}) %all-gather.11.cloned.1.call-update) | async-done | bytes 5242896 | tf_op jit(solution)/shard_map/all_gather | solution.py:225
  93.0 4.4 %fusion.14 = f32[256,1280]{1,0:T(8,128)S(1)} fusion(bf16[2048,1280]{1,0:T(8,128)(2,1)} %all-gather.11.cloned.1.call-done, bf16[256,2048]{1,0:T(8,128)(2,1)} %all-gather.9.cloned.1.call-done, f32[2048]{0:T(1024)S(1)} %copy-done.15, f32[256]{0:T(256)S(1)} %add_rsqrt_fusion.2), kind=kOutput, calls=%fused_computation.27 | convolution fusion | flops 1344274432 | bytes 7611392 | tf_op jit(solution)/shard_map/dot_general | solution.py:223
  100.0 0.8 fusion.5
  101.5 1.5 copy-done.14
  103.1 2.3 convolution_convert_fusion.1
  105.4 27.2 %reduce-scatter.4.cloned.1.call-done = bf16[64,2048]{1,0:T(8,128)(2,1)} async-done(((bf16[256,2048]{1,0:T(8,128)(2,1)}), bf16[64,2048]{1,0:T(8,128)(2,1)}) %reduce-scatter.4.cloned.1.call-update) | async-done | bytes 262160 | tf_op jit(solution)/shard_map/reduce_scatter | solution.py:309
  132.7 1.1 multiply_reduce_fusion.1
  133.8 1.8 multiply_convert_fusion
  135.7 26.7 %all-gather.19.cloned.1.call-done = bf16[256,2048]{1,0:T(8,128)(2,1)} async-done(((bf16[64,2048]{1,0:T(8,128)(2,1)}), bf16[256,2048]{1,0:T(8,128)(2,1)}) %all-gather.19.cloned.1.call-update) | async-done | bytes 1048592 | tf_op jit(solution)/shard_map/all_gather | solution.py:317
  162.6 3.2 convert_element_type.103
  165.8 5.0 %reshape.354 = bf16[8,2,64,2,4,192]{5,4,3,2,1,0:T(4,128)(2,1)} reshape(bf16[16,64,1536]{2,1,0:T(8,128)(2,1)S(1)} %convert_element_type.103) | data formatting | bytes 6291456 | tf_op jit(solution)/shard_map/reshape | solution.py:296
  170.8 9.0 %copy.60 = bf16[8,2,64,2,4,192]{5,1,3,2,4,0:T(2,128)(2,1)} copy(bf16[8,2,64,2,4,192]{5,4,3,2,1,0:T(4,128)(2,1)} %reshape.354) | data formatting | bytes 6291456 | tf_op jit(solution)/shard_map/reshape | solution.py:296
  179.8 9.0 %reshape.355 = bf16[32,64,768]{2,1,0:T(8,128)(2,1)S(1)} reshape(bf16[8,4,64,2,2,192]{5,4,3,2,1,0:T(2,128)(2,1)} %bitcast.87) | data formatting | bytes 6291456 | tf_op jit(solution)/shard_map/reshape | solution.py:298
  188.9 74.1 %all_to_all.22 = bf16[32,64,768]{2,1,0:T(8,128)(2,1)} all-to-all(bf16[32,64,768]{2,1,0:T(8,128)(2,1)S(1)} %reshape.355), channel_id=1, replica_groups=mesh['chip'=4,'core'=2,'tp'=4] {'chip','core','tp'}, dimensions={0} | all-to-all | bytes 6291456 | tf_op jit(solution)/shard_map/all_to_all | solution.py:300
  263.1 0.7 all-gather.17.cloned.1.call-update
  263.8 40.2 %all-gather.1 = s32[16,64,8]{1,2,0:T(8,128)S(1)} all-gather(s32[1,64,8]{1,2,0:T(8,128)S(1)} %bitcast.105), channel_id=1, replica_groups=mesh['chip'=4,'core'=2,'tp'=4] {'chip','tp'}, dimensions={0}, use_global_device_ids=true | all-gather | bytes 34816 | tf_op jit(solution)/shard_map/all_gather | solution.py:304
  304.3 3.4 fusion.48
  307.8 6.4 %fusion = f32[1024,768]{0,1:T(8,128)S(1)} fusion(bf16[1024,2048]{1,0:T(8,128)(2,1)} %bitcast.90, bf16[2,2048,768]{2,1,0:T(8,128)(2,1)} %all-gather.15.cloned.1.call-done), kind=kOutput, calls=%fused_computation.3 | convolution fusion | flops 3221225472 | bytes 10485760 | tf_op jit(solution)/shard_map/dot_general | solution.py:328
  314.2 3.6 fusion.1
  317.8 1.7 fusion.9
  319.5 6.9 %convolution_convert_fusion = bf16[1024,2048]{1,0:T(8,128)(2,1)} fusion(bf16[768,2048]{1,0:T(8,128)(2,1)} %bitcast.106, bf16[1024,384]{0,1:T(8,128)(2,1)S(1)} %get-tuple-element.19, bf16[1024,384]{0,1:T(8,128)(2,1)S(1)} %get-tuple-element.18), kind=kOutput, calls=%fused_computation.1 | convolution fusion | flops 3226468352 | bytes 8912896 | tf_op jit(solution)/shard_map/dot_general | solution.py:336
  326.5 50.1 %reduce-scatter.6.cloned.1.call-done = bf16[256,2048]{1,0:T(8,128)(2,1)} async-done(((bf16[1024,2048]{1,0:T(8,128)(2,1)}), bf16[256,2048]{1,0:T(8,128)(2,1)}) %reduce-scatter.6.cloned.1.call-update) | async-done | bytes 1048592 | tf_op jit(solution)/shard_map/reduce_scatter | solution.py:341
  377.3 1.3 iota_compare_fusion.3
  378.8 1.0 broadcast_select_fusion
  379.8 0.8 select_select_fusion
  380.6 25.5 %reduce-scatter.8.cloned.1.call-done = bf16[64,2048]{1,0:T(8,128)(2,1)} async-done(((bf16[256,2048]{1,0:T(8,128)(2,1)}), bf16[64,2048]{1,0:T(8,128)(2,1)}) %reduce-scatter.8.cloned.1.call-update) | async-done | bytes 262160 | tf_op jit(solution)/shard_map/reduce_scatter | solution.py:342
  406.1 1.8 select_convert_fusion
  (88 shorter events, 6.4 us)
Async XLA Ops:
  7.2 297.1 %copy-start = (bf16[2048,16]{0,1:T(8,128)(2,1)S(1)}, bf16[2048,16]{0,1:T(8,128)(2,1)}, u32[]{:S(2)}) copy-start(bf16[2048,16]{0,1:T(8,128)(2,1)} %param.20) | copy-start | bytes 196612
  7.2 43.7 %all-gather.9.cloned.1.call-start = ((), (), s32[]{:S(2)}) async-start(), calls=%async_computation.5 | async-start | bytes 1310720 | tf_op jit(solution)/shard_map/all_gather | solution.py:210
  7.9 85.1 %all-gather.11.cloned.1.call-start = ((), (), s32[]{:S(2)}) async-start(), calls=%async_computation.6 | async-start | bytes 5898240 | tf_op jit(solution)/shard_map/all_gather | solution.py:225
  10.2 82.9 %copy-start.15 = (f32[2048]{0:T(1024)S(1)}, f32[2048]{0:T(1024)}, u32[]{:S(2)}) copy-start(f32[2048]{0:T(1024)} %param.14) | copy-start | bytes 24580
  47.4 85.2 %reduce-scatter.4.cloned.1.call-start = ((), (), s32[]{:S(2)}) async-start(), calls=%async_computation.7 | async-start | bytes 1310720 | tf_op jit(solution)/shard_map/reduce_scatter | solution.py:309
  97.4 3.4 copy-start.5
  97.7 0.8 copy-start.11
  97.7 1.5 copy-start.12
  99.2 0.8 copy-start.6
  100.9 2.2 copy-start.14
  103.1 29.6 %copy-start.3 = (bf16[64,2048]{1,0:T(8,128)(2,1)S(1)}, bf16[64,2048]{1,0:T(8,128)(2,1)}, u32[]{:S(2)}) copy-start(bf16[64,2048]{1,0:T(8,128)(2,1)} %param.13) | copy-start | bytes 786436
  103.1 30.8 %copy-start.8 = (f32[2048]{0:T(1024)S(1)}, f32[2048]{0:T(1024)}, u32[]{:S(2)}) copy-start(f32[2048]{0:T(1024)} %param.19) | copy-start | bytes 24580
  105.4 57.0 %all-gather.19.cloned.1.call-start = ((), (), s32[]{:S(2)}) async-start(), calls=%async_computation.13 | async-start | bytes 1310720 | tf_op jit(solution)/shard_map/all_gather | solution.py:317
  135.6 168.6 %all-gather.13.cloned.1.call-start = ((), (), s32[]{:S(2)}) async-start(), calls=%async_computation.8 | async-start | bytes 5242880 | tf_op jit(solution)/shard_map/all_gather | solution.py:318
  162.4 145.4 %all-gather.15.cloned.1.call-start = ((), (), s32[]{:S(2)}) async-start(), calls=%async_computation.9 | async-start | bytes 9437184 | tf_op jit(solution)/shard_map/all_gather | solution.py:302
  263.0 0.8 copy-start.9
  263.0 56.5 %all-gather.17.cloned.1.call-start = ((), (), s32[]{:S(2)}) async-start(), calls=%async_computation.10 | async-start | bytes 4718592 | tf_op jit(solution)/shard_map/all_gather | solution.py:303
  263.8 112.9 %reduce-scatter.6.cloned.1.call-start = ((), (), s32[]{:S(2)}) async-start(), calls=%async_computation.11 | async-start | bytes 5242880 | tf_op jit(solution)/shard_map/reduce_scatter | solution.py:341
  307.7 6.4 %copy-start.2 = (bf16[16,64,2048]{2,1,0:T(8,128)(2,1)S(1)}, bf16[16,64,2048]{2,1,0:T(8,128)(2,1)}, u32[]{:S(2)}) copy-start(bf16[16,64,2048]{2,1,0:T(8,128)(2,1)} %all-gather.13.cloned.1.call-done) | copy-start | bytes 12582916
  307.8 6.4 %copy-start.13 = (bf16[2,2048,768]{2,1,0:T(8,128)(2,1)S(1)}, bf16[2,2048,768]{2,1,0:T(8,128)(2,1)}, u32[]{:S(2)}) copy-start(bf16[2,2048,768]{2,1,0:T(8,128)(2,1)} %all-gather.15.cloned.1.call-done) | copy-start | bytes 18874372
  326.4 50.2 %copy-start.10 = (s32[1,2]{1,0:T(1,128)S(1)}, s32[1,2]{1,0:T(1,128)}, u32[]{:S(2)}) copy-start(s32[1,2]{1,0:T(1,128)} %param.25) | copy-start | bytes 28
  326.4 52.2 %copy-start.7 = (bf16[256,1,64]{2,0,1:T(8,128)(2,1)S(1)}, bf16[256,1,64]{2,0,1:T(8,128)(2,1)}, u32[]{:S(2)}) copy-start(bf16[256,1,64]{2,0,1:T(8,128)(2,1)} %copy-done.6) | copy-start | bytes 98308
  326.5 79.6 %copy-start.4 = (bf16[64,2048]{1,0:T(8,128)(2,1)S(1)}, bf16[64,2048]{1,0:T(8,128)(2,1)}, u32[]{:S(2)}) copy-start(bf16[64,2048]{1,0:T(8,128)(2,1)} %reduce-scatter.4.cloned.1.call-done) | copy-start | bytes 786436
  326.5 81.4 %copy-start.1 = (bf16[2048,16]{0,1:T(8,128)(2,1)S(1)}, bf16[2048,16]{0,1:T(8,128)(2,1)}, u32[]{:S(2)}) copy-start(bf16[2048,16]{0,1:T(8,128)(2,1)} %param.20) | copy-start | bytes 196612
  326.5 79.6 %reduce-scatter.8.cloned.1.call-start = ((), (), s32[]{:S(2)}) async-start(), calls=%async_computation.12 | async-start | bytes 1310720 | tf_op jit(solution)/shard_map/reduce_scatter | solution.py:342
Sparse Core Ops, SparseCore 0:
  9.6 41.2 all-gather.8
  52.8 40.2 all-gather.10
  105.5 27.1 reduce-scatter.3
  135.7 26.5 all-gather.18
  164.2 80.6 all-gather.12
  263.1 16.6 all-gather.14
  281.4 13.2 all-gather.16
  326.6 49.9 reduce-scatter.5
  378.9 27.1 reduce-scatter.7

commit v2 on v1

--- a/solution.py
+++ b/solution.py
@@ -1,8 +1,11 @@
+import functools
 import math
 
 import jax
 import jax.numpy as jnp
 from jax import lax
+from jax.experimental import pallas as pl
+from jax.experimental.pallas import tpu as pltpu
 from jax.sharding import Mesh, PartitionSpec as P
 
 QUERY_HEADS = 32
@@ -201,8 +204,153 @@
 DENSE_BYTES = 16 << 20
 
 
+def place_of(index, tensor_parallel_count):
+    seq_index = index // tensor_parallel_count
+    return (seq_index // 2, seq_index % 2, index % tensor_parallel_count)
+
+
+def weights_kernel(
+    chips, tensors, query_width, key_width, rounded, gate_up, down, columns, pair_gate_up,
+    pair_down, send, recv, local,
+):
+    chip, core, tp = lax.axis_index("chip"), lax.axis_index("core"), lax.axis_index("tp")
+    seq = chip * 2 + core
+    me = seq * tensors + tp
+    total = chips * 2 * tensors
+    partner = (chip, 1 - core, tp)
+    rows = rounded.shape[0]
+    prompt = rows * tensors
+    exp_here = pair_gate_up.shape[1]
+    block = pair_gate_up.shape[3]
+    key_start = query_width * tensors
+    pieces = (
+        (0, query_width, 0),
+        (key_start, key_width, query_width),
+        (key_start + key_width * tensors, key_width, query_width + key_width),
+    )
+
+    def remote(source, target, number, device):
+        return pltpu.make_async_remote_copy(
+            src_ref=source,
+            dst_ref=target,
+            send_sem=send.at[number],
+            recv_sem=recv.at[number],
+            device_id=device,
+            device_id_type=pl.DeviceIdType.MESH,
+        )
+
+    def wait(reference, semaphore):
+        pltpu.make_async_copy(reference, reference, semaphore).wait()
+
+    barrier = pltpu.get_barrier_semaphore()
+
+    @pl.loop(1, total)
+    def _(step):
+        pl.semaphore_signal(
+            barrier,
+            inc=1,
+            device_id=place_of((me + step) % total, tensors),
+            device_id_type=pl.DeviceIdType.MESH,
+        )
+
+    pl.semaphore_wait(barrier, total - 1)
+
+    own_rows = pl.ds(pl.multiple_of(me * rows, rows), rows)
+
+    def column_parts(target_tp):
+        for start, size, landing in pieces:
+            yield (
+                rounded.at[:, pl.ds(pl.multiple_of(start + target_tp * size, 128), size)],
+                columns.at[own_rows, pl.ds(landing, size)],
+            )
+
+    def unit_part(target_seq, target_tp, target_core):
+        return (
+            gate_up.at[
+                pl.ds(target_seq * exp_here, exp_here),
+                :,
+                pl.ds(pl.multiple_of(target_tp * block, 128), block),
+            ],
+            pair_gate_up.at[target_core, :, own_rows, :],
+        )
+
+    for step in range(1, tensors):
+        target_tp = (tp + step) % tensors
+        for source, target in column_parts(target_tp):
+            remote(source, target, 0, (chip, core, target_tp)).start()
+    for source, target in column_parts(tp):
+        pltpu.make_async_copy(source, target, local.at[0]).start()
+    pltpu.make_async_copy(*unit_part(seq, tp, core), local.at[1]).start()
+    pltpu.make_async_copy(down, pair_down.at[core], local.at[2]).start()
+
+    @pl.loop(1, total)
+    def _(step):
+        place = place_of((me + step) % total, tensors)
+        source, target = unit_part(place[0] * 2 + place[1], place[2], place[1])
+        remote(source, target, 1, place).start()
+
+    remote(down, pair_down.at[core], 2, partner).start()
+
+    wait(columns.at[pl.ds(0, prompt - rows)], recv.at[0])
+    wait(columns.at[pl.ds(0, rows)], local.at[0])
+
+    def prompt_part(chip_index):
+        start = pl.multiple_of((chip_index * 2 + core) * prompt, prompt)
+        return columns.at[pl.ds(start, prompt)]
+
+    for step in range(1, chips):
+        remote(prompt_part(chip), prompt_part(chip), 3, ((chip + step) % chips, core, tp)).start()
+    remote(prompt_part(chip), prompt_part(chip), 4, partner).start()
+    wait(columns.at[pl.ds(0, (chips - 1) * prompt)], recv.at[3])
+    for step in range(1, chips):
+        other = (chip + step) % chips
+        remote(prompt_part(other), prompt_part(other), 4, partner).start()
+
+    wait(pair_gate_up.at[0, :, pl.ds(0, (total - 1) * rows), :], recv.at[1])
+    wait(pair_gate_up.at[0, :, pl.ds(0, rows), :], local.at[1])
+    remote(pair_gate_up.at[core], pair_gate_up.at[core], 5, partner).start()
+
+    wait(columns.at[pl.ds(0, chips * prompt)], recv.at[4])
+    wait(pair_down.at[0], recv.at[2])
+    wait(pair_down.at[0], local.at[2])
+    wait(pair_gate_up.at[0], recv.at[5])
+    wait(columns.at[pl.ds(0, prompt - rows)], send.at[0])
+    wait(pair_gate_up.at[0, :, pl.ds(0, (total - 1) * rows), :], send.at[1])
+    wait(pair_down.at[0], send.at[2])
+    wait(columns.at[pl.ds(0, (chips - 1) * prompt)], send.at[3])
+    wait(columns.at[pl.ds(0, chips * prompt)], send.at[4])
+    wait(pair_gate_up.at[0], send.at[5])
+
+
+def move_weights(rounded, gate_up, down):
+    chips, tensors = lax.axis_size("chip"), lax.axis_size("tp")
+    rows = rounded.shape[0]
+    all_rows = rows * chips * 2 * tensors
+    exp_here = gate_up.shape[0] // (chips * 2)
+    block = gate_up.shape[2] // tensors
+    query_width = QUERY_HEADS * HEAD_SIZE // tensors
+    key_width = KEY_VALUE_HEADS * HEAD_SIZE // tensors
+    anywhere = pl.BlockSpec(memory_space=pl.ANY)
+    return pl.pallas_call(
+        functools.partial(weights_kernel, chips, tensors, query_width, key_width),
+        out_shape=(
+            jax.ShapeDtypeStruct((all_rows, query_width + 2 * key_width), jnp.bfloat16),
+            jax.ShapeDtypeStruct((2, exp_here, all_rows, block), jnp.bfloat16),
+            jax.ShapeDtypeStruct((2,) + down.shape, jnp.bfloat16),
+        ),
+        in_specs=[anywhere] * 3,
+        out_specs=(anywhere,) * 3,
+        scratch_shapes=[
+            pltpu.SemaphoreType.DMA((6,)),
+            pltpu.SemaphoreType.DMA((6,)),
+            pltpu.SemaphoreType.DMA((3,)),
+        ],
+        compiler_params=pltpu.CompilerParams(collective_id=0, has_side_effects=True),
+    )(rounded, gate_up, down)
+
+
 def project_and_attend(
-    hidden_in, attention_gain, attention_trainer_copy, query_gain, key_gain, prompt_length
+    hidden_in, attention_gain, attention_columns, query_gain, key_gain, prompt_length
 ):
     tensor_parallel_count = lax.axis_size("tp")
     heads_here = QUERY_HEADS // tensor_parallel_count
@@ -210,19 +358,9 @@
     prompt_rows = lax.all_gather(hidden_in, "tp", axis=0, tiled=True)
     column_span = prompt_rows.shape[0]
     normed = rms_scale(prompt_rows.astype(jnp.float32), attention_gain).astype(jnp.bfloat16)
-    trainer_rows = attention_trainer_copy.shape[0]
-    query_end = QUERY_HEADS * HEAD_SIZE
-    key_end = query_end + KEY_VALUE_HEADS * HEAD_SIZE
-    rounded = attention_trainer_copy.astype(jnp.bfloat16)
-    parts = [
-        part.reshape(trainer_rows, tensor_parallel_count, -1)
-        for part in (rounded[:, :query_end], rounded[:, query_end:key_end], rounded[:, key_end:])
-    ]
-    joined = jnp.concatenate(parts, axis=2).reshape(trainer_rows, -1)
-    head_rows = lax.all_to_all(joined, "tp", split_axis=1, concat_axis=0, tiled=True)
     projected_rows = jnp.dot(
         normed,
-        lax.all_gather(head_rows, PLANE, axis=0, tiled=True),
+        attention_columns,
         preferred_element_type=jnp.float32,
     )
     positions = jnp.arange(column_span)
@@ -290,21 +428,24 @@
     exp_here = experts_all // seq_count
     units_here = FF // tensor_parallel_count
     prompt_length = lengths[0]
-    master_rows = gate_up_master.shape[1]
-    blocks = (
-        gate_up_master.astype(jnp.bfloat16)
-        .reshape(seq_count, exp_here, master_rows, 2, tensor_parallel_count, units_here)
-        .transpose(0, 4, 2, 3, 1, 5)
-        .reshape(seq_count * tensor_parallel_count, master_rows, 2 * exp_here * units_here)
-    )
-    mine = lax.all_to_all(blocks, EVERY, split_axis=0, concat_axis=0, tiled=True)
-    mine = mine.reshape(-1, 2 * exp_here * units_here)
-    pair_gate_up = lax.all_gather(mine, "core", axis=0)
-    pair_down = lax.all_gather(down_weight.reshape(-1, width), "core", axis=0)
+    column = jnp.arange(2 * FF)
+    quarter_of, within = column // (2 * units_here), column % (2 * units_here)
+    origin = (within // units_here) * FF + quarter_of * units_here + within % units_here
+    selector = (column[:, None] == origin[None, :]).astype(jnp.bfloat16)
+    ordered = jnp.dot(
+        gate_up_master.astype(jnp.bfloat16).reshape(-1, 2 * FF),
+        selector,
+        preferred_element_type=jnp.float32,
+    ).astype(jnp.bfloat16)
+    attention_columns, pair_gate_up, pair_down = move_weights(
+        attention_trainer_copy.astype(jnp.bfloat16),
+        ordered.reshape(gate_up_master.shape),
+        down_weight.reshape(-1, width),
+    )
     pair_routes = lax.all_gather(routes, ROWS, axis=0, tiled=True)
 
     context_rows, keys_rotated, values_rows = project_and_attend(
-        hidden_in, attention_gain, attention_trainer_copy, query_gain, key_gain, prompt_length
+        hidden_in, attention_gain, attention_columns, query_gain, key_gain, prompt_length
     )
     attention_sums = lax.psum_scatter(
         jnp.dot(context_rows, output_proj, preferred_element_type=jnp.float32).astype(jnp.bfloat16),
@@ -322,19 +463,16 @@
     raised = jnp.where(named, jnp.exp(logits), 0.0)
     gates = raised / jnp.sum(raised, axis=1, keepdims=True)
     chip_gates = lax.dynamic_slice_in_dim(gates, chip_place * 2 * exp_here, 2 * exp_here, axis=1)
-    column_expert = jnp.arange(exp_here * units_here) // units_here
-    halves = []
+    pieces = []
     for core in range(2):
-        both = jnp.dot(group_rows, pair_gate_up[core], preferred_element_type=jnp.float32)
-        spread = jnp.zeros((group_rows.shape[0], exp_here * units_here), jnp.float32)
         for slot in range(exp_here):
+            weights = pair_gate_up[core, slot]
+            both = jnp.dot(group_rows, weights, preferred_element_type=jnp.float32)
+            units = jax.nn.silu(both[:, :units_here]) * both[:, units_here:]
             gate = chip_gates[:, core * exp_here + slot][:, None]
-            spread = jnp.where(column_expert[None, :] == slot, gate, spread)
-        hidden_units = exp_here * units_here
-        units = jax.nn.silu(both[:, :hidden_units]) * both[:, hidden_units:] * spread
-        halves.append(units.astype(jnp.bfloat16))
+            pieces.append((units * gate).astype(jnp.bfloat16))
     partial = jnp.dot(
-        jnp.concatenate(halves, axis=1),
+        jnp.concatenate(pieces, axis=1),
         pair_down.reshape(-1, width),
         preferred_element_type=jnp.float32,
     ).astype(jnp.bfloat16)

time: 415 us -> 365 us (0.88)
  blocking collectives: 151 us -> 40.3 us
  Pallas kernels: 0 us -> 105 us
  waiting for transfers between devices: 174 us -> 149 us
  local copies, waits for them, and re-layouts: 26.4 us -> 4.19 us
  matrix products: 28.4 us -> 32.8 us
    all_to_all x2 -> x0, blocking collectives: 111 us -> none  [the longest x1 74.1 us: on_device(): lax.all_to_all(blocks, EVERY, split_axis=0, concat_axis=0, tiled=True)]
    pallas_call x0 -> x1, Pallas kernels: none -> 105 us  [move_weights(): pl.pallas_call(functools.partial(weights_kernel, chips, tensors, query_wi...]
    all_gather x3 -> x0, waiting for transfers between devices: 40.7 us -> none  [the longest x1 40.6 us: project_and_attend(): lax.all_gather(head_rows, PLANE, axis=0, tiled=True)]
    reshape x6 -> x0, local copies, waits for them, and re-layouts: 23.4 us -> none  [the longest x3 23 us: on_device(): blocks = gate_up_master.astype(jnp.bfloat16).reshape(seq_count, exp_here,...]
    all_gather x1, waiting for transfers between devices: 0.02 us -> 14 us  [on_device(): lax.all_gather(group_rows, 'chip', axis=0, tiled=True).reshape(-1, width)]
    dot_general x4 -> x7, matrix products: 21.3 us -> 27.8 us  [the longest x4 11.7 us: on_device(): both = jnp.dot(group_rows, weights, preferred_element_type=jnp.float32)]
  transfers between devices with their start and end apart: 9 -> 6, of which waited for: 6 -> 5; matrix products, arithmetic and copies ran while one was open for 12% -> 4% of each run, Pallas kernels for 0% -> 29%
where the time goes in v2:
time: 365 us
  waiting for transfers between devices  149 us (41%)
  Pallas kernels  105 us (29%)
  blocking collectives  40.3 us (11%)
  matrix products  32.8 us (9%)
  other arithmetic  17.7 us (5%)
  between operations  15.2 us (4%)
  local copies, waits for them, and re-layouts  4.19 us (1%)
    pallas_call x1, Pallas kernels, move_weights(): pl.pallas_call(functools.partial(weights_kernel, chips, tensors, query_wi...  105 us
    reduce_scatter x1, waiting for transfers between devices, on_device(): lax.psum_scatter(partial, 'chip', scatter_dimension=0, tiled=True)  52.7 us
    all_gather x1, blocking collectives, on_device(): pair_routes = lax.all_gather(routes, ROWS, axis=0, tiled=True)  40.3 us
    reduce_scatter x1, waiting for transfers between devices, on_device(): lax.psum_scatter(jnp.dot(context_rows, output_proj, preferred_element_typ...  28.5 us
    all_gather x1, waiting for transfers between devices, on_device(): group_rows = lax.all_gather(mixed, 'tp', axis=0, tiled=False)  26.7 us
    reduce_scatter x1, waiting for transfers between devices, on_device(): combined = lax.psum_scatter(combined, 'tp', scatter_dimension=0, tiled=True)  26.3 us
    all_gather x1, waiting for transfers between devices, on_device(): lax.all_gather(group_rows, 'chip', axis=0, tiled=True).reshape(-1, width)  14 us
    dot_general x4, matrix products, on_device(): both = jnp.dot(group_rows, weights, preferred_element_type=jnp.float32)  11.7 us
  transfers between devices with their start and end apart: 6, of which 5 were waited for; matrix products, arithmetic and copies ran while one was open for 4% of the time, Pallas kernels for 29%

profile of v2, /device:TPU:0, one launch (start us, length us, event | category | flops | bytes accessed | tf_op | source)
XLA Modules:
  0.0 364.7 jit_solution(1388445655116409729)
XLA Ops:
  7.2 0.7 all-gather.6.cloned.1.call-update
  8.0 2.2 convert_element_type.107.rounded
  10.2 3.2 convert_element_type.108
  14.1 6.7 %fusion.2 = bf16[1536,1024]{0,1:T(8,128)(2,1)} fusion(bf16[1024,1536]{1,0:T(8,128)(2,1)S(1)} %bitcast.100, s32[1536]{0:T(1024)S(1)} %fusion.67), kind=kOutput, calls=%fused_computation.3 | convolution fusion | flops 4835770368 | bytes 6297600 | tf_op jit(solution)/shard_map/dot_general | solution.py:435
  20.8 105.4 %shard_map.140 = (bf16[2048,1280]{1,0:T(8,128)(2,1)}, bf16[2,2,2048,384]{3,2,1,0:T(8,128)(2,1)}, bf16[2,384,2048]{2,1,0:T(8,128)(2,1)}) custom-call(bf16[64,5120]{1,0:T(8,128)(2,1)} %convert_element_type.107.rounded, bf16[16,64,1536]{2,1,0:T(8,128)(2,1)} %bitcast.99, bf16[384,2048]{1,0:T(8,128)(2,1)} %bitcast.101), custom_call_target="tpu_custom_call" | custom-call | tf_op jit(solution)/shard_map/pallas_call | solution.py:334
  126.4 0.5 multiply_cosine_fusion
  127.0 1.5 fusion.3
  128.5 4.4 %fusion.27 = f32[256,1280]{1,0:T(8,128)S(1)} fusion(bf16[2048,1280]{1,0:T(8,128)(2,1)} %get-tuple-element.5, bf16[256,2048]{1,0:T(8,128)(2,1)} %all-gather.6.cloned.1.call-done, f32[2048]{0:T(1024)S(1)} %copy-done.11, f32[256]{0:T(256)S(1)} %add_rsqrt_fusion.2), kind=kOutput, calls=%fused_computation.36 | convolution fusion | flops 1344274432 | bytes 7611392 | tf_op jit(solution)/shard_map/dot_general | solution.py:361
  134.0 0.6 fusion.53
  135.4 0.8 fusion.6
  136.3 0.7 convolution_convert_fusion.2
  136.9 1.5 copy-done.9
  138.5 2.3 convolution_convert_fusion.1
  140.8 28.5 %reduce-scatter.4.cloned.1.call-done = bf16[64,2048]{1,0:T(8,128)(2,1)} async-done(((bf16[256,2048]{1,0:T(8,128)(2,1)}), bf16[64,2048]{1,0:T(8,128)(2,1)}) %reduce-scatter.4.cloned.1.call-update) | async-done | bytes 262160 | tf_op jit(solution)/shard_map/reduce_scatter | solution.py:450
  169.3 1.1 multiply_reduce_fusion.1
  170.5 1.8 multiply_convert_fusion
  172.3 26.7 %all-gather.10.cloned.1.call-done = bf16[256,2048]{1,0:T(8,128)(2,1)} async-done(((bf16[64,2048]{1,0:T(8,128)(2,1)}), bf16[256,2048]{1,0:T(8,128)(2,1)}) %all-gather.10.cloned.1.call-update) | async-done | bytes 1048592 | tf_op jit(solution)/shard_map/all_gather | solution.py:458
  199.1 40.3 %all-gather.1 = s32[16,64,8]{1,2,0:T(8,128)S(1)} all-gather(s32[1,64,8]{1,2,0:T(8,128)S(1)} %bitcast.112), channel_id=1, replica_groups=mesh['chip'=4,'core'=2,'tp'=4] {'chip','tp'}, dimensions={0}, use_global_device_ids=true | all-gather | bytes 34816 | tf_op jit(solution)/shard_map/all_gather | solution.py:445
  239.5 14.0 %all-gather.8.cloned.1.call-done = bf16[16,64,2048]{2,1,0:T(8,128)(2,1)} async-done(((bf16[4,64,2048]{2,1,0:T(8,128)(2,1)}), bf16[16,64,2048]{2,1,0:T(8,128)(2,1)}) %all-gather.8.cloned.1.call-update) | async-done | bytes 4194320 | tf_op jit(solution)/shard_map/all_gather | solution.py:459
  253.5 4.6 %fusion.14 = f32[1024,384]{0,1:T(8,128)S(1)} fusion(bf16[1024,2048]{1,0:T(8,128)(2,1)} %bitcast.93, bf16[2,2,2048,384]{3,2,1,0:T(8,128)(2,1)} %get-tuple-element.6), kind=kOutput, calls=%fused_computation.21 | convolution fusion | flops 1610612736 | bytes 7340032 | tf_op jit(solution)/shard_map/dot_general | solution.py:470
  258.1 3.4 fusion.16
  261.6 1.8 fusion.18
  263.4 1.8 fusion.20
  265.2 1.2 fusion.84
  267.5 1.4 copy-done.10
  268.9 5.1 %convolution_convert_fusion = bf16[1024,2048]{1,0:T(8,128)(2,1)} fusion(bf16[768,2048]{1,0:T(8,128)(2,1)S(1)} %bitcast.115, bf16[1024,192]{0,1:T(8,128)(2,1)S(1)} %get-tuple-element.28, bf16[1024,192]{0,1:T(8,128)(2,1)S(1)} %get-tuple-element.29, bf16[1024,192]{0,1:T(8,128)(2,1)S(1)} %get-tuple-element.30, bf16[1024,192]{0,1:T(8,128)(2,1)S(1)} %get-tuple-element.31), kind=kOutput, calls=%fused_computation.4 | convolution fusion | flops 3229614080 | bytes 8912896 | tf_op jit(solution)/shard_map/dot_general | solution.py:474
  274.0 52.7 %reduce-scatter.6.cloned.1.call-done = bf16[256,2048]{1,0:T(8,128)(2,1)} async-done(((bf16[1024,2048]{1,0:T(8,128)(2,1)}), bf16[256,2048]{1,0:T(8,128)(2,1)}) %reduce-scatter.6.cloned.1.call-update) | async-done | bytes 1048592 | tf_op jit(solution)/shard_map/reduce_scatter | solution.py:479
  326.8 0.6 fusion.83
  327.4 1.3 iota_compare_fusion.7
  329.0 0.8 select_select_fusion
  329.8 26.3 %reduce-scatter.8.cloned.1.call-done = bf16[64,2048]{1,0:T(8,128)(2,1)} async-done(((bf16[256,2048]{1,0:T(8,128)(2,1)}), bf16[64,2048]{1,0:T(8,128)(2,1)}) %reduce-scatter.8.cloned.1.call-update) | async-done | bytes 262160 | tf_op jit(solution)/shard_map/reduce_scatter | solution.py:480
  356.1 1.8 select_convert_fusion
  (69 shorter events, 3.9 us)
Async XLA Ops:
  7.2 258.1 %copy-start = (bf16[2048,16]{0,1:T(8,128)(2,1)S(1)}, bf16[2048,16]{0,1:T(8,128)(2,1)}, u32[]{:S(2)}) copy-start(bf16[2048,16]{0,1:T(8,128)(2,1)} %param.20) | copy-start | bytes 196612
  7.2 119.8 %all-gather.6.cloned.1.call-start = ((), (), s32[]{:S(2)}) async-start(), calls=%async_computation.3 | async-start | bytes 1310720 | tf_op jit(solution)/shard_map/all_gather | solution.py:358
  7.9 161.4 %reduce-scatter.4.cloned.1.call-start = ((), (), s32[]{:S(2)}) async-start(), calls=%async_computation.4 | async-start | bytes 1310720 | tf_op jit(solution)/shard_map/reduce_scatter | solution.py:450
  20.8 107.7 %copy-start.11 = (f32[2048]{0:T(1024)S(1)}, f32[2048]{0:T(1024)}, u32[]{:S(2)}) copy-start(f32[2048]{0:T(1024)} %param.14) | copy-start | bytes 24580
  133.2 0.8 copy-start.7
  133.2 1.5 copy-start.8
  136.3 2.2 copy-start.9
  138.5 30.8 %copy-start.2 = (bf16[64,2048]{1,0:T(8,128)(2,1)S(1)}, bf16[64,2048]{1,0:T(8,128)(2,1)}, u32[]{:S(2)}) copy-start(bf16[64,2048]{1,0:T(8,128)(2,1)} %param.13) | copy-start | bytes 786436
  138.5 32.0 %copy-start.4 = (f32[2048]{0:T(1024)S(1)}, f32[2048]{0:T(1024)}, u32[]{:S(2)}) copy-start(f32[2048]{0:T(1024)} %param.19) | copy-start | bytes 24580
  140.7 58.3 %copy-start.5 = (s32[64,8]{0,1:T(8,128)S(1)}, s32[64,8]{0,1:T(8,128)}, u32[]{:S(2)}) copy-start(s32[64,8]{0,1:T(8,128)} %param.23) | copy-start | bytes 6148
  140.8 58.2 %all-gather.10.cloned.1.call-start = ((), (), s32[]{:S(2)}) async-start(), calls=%async_computation.8 | async-start | bytes 1310720 | tf_op jit(solution)/shard_map/all_gather | solution.py:458
  172.2 81.2 %all-gather.8.cloned.1.call-start = ((), (), s32[]{:S(2)}) async-start(), calls=%async_computation.5 | async-start | bytes 5242880 | tf_op jit(solution)/shard_map/all_gather | solution.py:459
  199.0 127.7 %reduce-scatter.6.cloned.1.call-start = ((), (), s32[]{:S(2)}) async-start(), calls=%async_computation.6 | async-start | bytes 5242880 | tf_op jit(solution)/shard_map/reduce_scatter | solution.py:479
  253.5 4.7 %copy-start.1 = (bf16[16,64,2048]{2,1,0:T(8,128)(2,1)S(1)}, bf16[16,64,2048]{2,1,0:T(8,128)(2,1)}, u32[]{:S(2)}) copy-start(bf16[16,64,2048]{2,1,0:T(8,128)(2,1)} %all-gather.8.cloned.1.call-done) | copy-start | bytes 12582916
  253.5 8.1 %slice-start = ((s8[6291456]{0:T(1024)(128)(4,1)}), s8[4194304]{0:T(1024)(128)(4,1)S(1)}, s32[]{:S(2)}) async-start(s8[6291456]{0:T(1024)(128)(4,1)} %bitcast.113), calls=%async_computation.9 | async-start | bytes 8388608
  258.1 3.4 slice-start.1
  267.0 1.9 copy-start.10
  274.0 52.9 %copy-start.6 = (s32[1,2]{1,0:T(1,128)S(1)}, s32[1,2]{1,0:T(1,128)}, u32[]{:S(2)}) copy-start(s32[1,2]{1,0:T(1,128)} %param.25) | copy-start | bytes 28
  274.0 82.1 %copy-start.3 = (bf16[64,2048]{1,0:T(8,128)(2,1)S(1)}, bf16[64,2048]{1,0:T(8,128)(2,1)}, u32[]{:S(2)}) copy-start(bf16[64,2048]{1,0:T(8,128)(2,1)} %reduce-scatter.4.cloned.1.call-done) | copy-start | bytes 786436
  274.0 82.1 %reduce-scatter.8.cloned.1.call-start = ((), (), s32[]{:S(2)}) async-start(), calls=%async_computation.7 | async-start | bytes 1310720 | tf_op jit(solution)/shard_map/reduce_scatter | solution.py:480
Sparse Core Ops, SparseCore 0:
  9.6 47.8 all-gather.5
  140.9 28.3 reduce-scatter.3
  172.4 26.5 all-gather.9
  200.8 52.5 all-gather.7
  274.1 52.6 reduce-scatter.5
  328.9 27.1 reduce-scatter.7
